TPU v7x, 32 devices: a whole 2x2x4 slice. The times are simulated.
32 devices in a mesh: gx: 4 (over z), gy: 4 (over x, core), gz: 2 (over y).
Axes of the slice: x: 2, y: 2, z: 4, core: 2. Of those that a mesh axis runs over, the one named last changes fastest.
Arguments:
- velocity: float32 [3, 64, 32, 256], P(None, 'gx', 'gy', 'gz'), may hold values from -6 to 6
- acoustic: float32 [1024, 4, 512], P(('gx', 'gy', 'gz')), may hold values from -6 to 6
- projection: float32 [64, 512], replicated, may hold values from -0.75 to 0.75
- owner_index: int32 [1024, 1], P(('gx', 'gy', 'gz')), may hold values from 0 to 7; in each aligned block of 32 rows (0 to 31, 32 to 63, ...) at most 8 rows name the same one
- slot_element: int32 [32, 64], P(('gx', 'gy', 'gz')), may hold values from 0 to 31
- element_cell: int32 [32, 32], P(('gx', 'gy', 'gz')), may hold values from 0 to 31, each once within a row
Outputs:
- velocity_out: float32 [3, 64, 32, 256], P(None, 'gx', 'gy', 'gz')
- acoustic_out: float32 [1024, 4, 512], P(('gx', 'gy', 'gz'))
Inputs may be any that keep to these rules, and one draw needn't show every extreme that they name: `owner_index`: owners are numbered gy index times 2 plus gz index within the sender's gx plane; among one device's 32 rows no owner appears more than 8 times. Slot q of a device feeds its stored element slot_element[q]. `element_cell`: each row is a permutation of the brick cells of one device.
All inputs are finite; a program needn't handle non-finite values.
Results may differ from a plain program's by a relative error of at most 0.0019.
Values may be sent and summed in bfloat16 or wider, within the bound.
A program may use at most 128 MiB of HBM per device.

v0:
```python
import functools

import jax
import jax.numpy as jnp
import numpy as np
from jax import lax
from jax.experimental import pallas as pl
from jax.experimental.pallas import tpu as pltpu
from jax.sharding import PartitionSpec as P

VS = 4
ORDER = 7
EBX = 1
EBY = 2
EBZ = 16
K = ORDER + 1
FACE = K * K
NODES = K**3

HIGHEST = lax.Precision.HIGHEST
FLOW_STEP = 0.1
VISCOSITY = 0.05
WAVE_STEP = 0.02
SOURCE_GAIN = 25.0
MESH = pl.DeviceIdType.MESH


def legendre_table(points, order):
    columns = [points * 0.0 + 1.0, points]
    for degree in range(2, order + 1):
        columns.append(
            ((2 * degree - 1) * points * columns[degree - 1] - (degree - 1) * columns[degree - 2])
            / degree
        )
    return np.stack(columns, axis=1)


def lobatto_tables(order):
    point_count = order + 1
    points = -np.cos(np.pi * np.arange(point_count) / order)
    for newton_step in range(60):
        legendre = legendre_table(points, order)
        points = points - (points * legendre[:, order] - legendre[:, order - 1]) / (
            point_count * legendre[:, order]
        )
    legendre = legendre_table(points, order)
    highest = legendre[:, order]
    spacing = points[:, None] - points[None, :] + np.eye(point_count)
    derivative = highest[:, None] / (highest[None, :] * spacing)
    derivative = derivative * (1.0 - np.eye(point_count))
    derivative[0, 0] = -order * point_count / 4.0
    derivative[order, order] = order * point_count / 4.0
    return derivative


def iota(shape, axis):
    return lax.broadcasted_iota(jnp.int32, shape, axis)


def as_float(mask):
    return jnp.where(mask, 1.0, 0.0).astype(jnp.float32)


def to_column(row, count):
    eye = iota((count, count), 0) == iota((count, count), 1)
    return jnp.sum(jnp.where(eye, row, 0.0), axis=1, keepdims=True)


def to_row(column, count):
    eye = iota((count, count), 0) == iota((count, count), 1)
    return jnp.sum(jnp.where(eye, column, 0.0), axis=0, keepdims=True)


def spread_row(column, count, width, group):
    pick = iota((count, width), 0) == iota((count, width), 1) // group
    return jnp.sum(jnp.where(pick, column, 0.0), axis=0, keepdims=True)


def split(value):
    high = value.astype(jnp.bfloat16)
    low = (value - high.astype(jnp.float32)).astype(jnp.bfloat16)
    return high, low


def dot(a, b, contract=((1,), (0,)), precision=None):
    return lax.dot_general(
        a, b, (contract, ((), ())), preferred_element_type=jnp.float32, precision=precision
    )


def swap(value, group, along, width):
    axis = value.ndim - 1
    total = 4 * width
    here = (1 + along) * width
    up = pltpu.roll(value, here, axis)
    down = up if 2 * here == total else pltpu.roll(value, total - here, axis)
    return jnp.where(group == 0, down, jnp.where(group == 1 + along, up, 0.0))


def derive(values, table):
    half = K // 2
    even = [values[j] + values[K - 1 - j] for j in range(half)]
    odd = [values[j] - values[K - 1 - j] for j in range(half)]
    result = [None] * K
    for a in range(half):
        first = sum(
            float(0.5 * (table[a, j] - table[a, K - 1 - j])) * odd[j] for j in range(half)
        )
        second = sum(
            float(0.5 * (table[a, j] + table[a, K - 1 - j])) * even[j] for j in range(half)
        )
        result[a] = first + second
        result[K - 1 - a] = first - second
    return result


def kernel(
    sizes,
    u_in, ac_in, proj_in, owner_in, slot_in, cell_in,
    u_out, ac_out,
    flow, y_send, y_recv, z_send, z_recv, tr_send, tr_recv, vol_send, vol_recv,
    q_ref, acc, lhs, place, gather, proj_ref,
    v_ssem, v_rsem, t_ssem, t_rsem, p_ssem, p_rsem,
):
    nx, ny, nz, X, Y, Z, E, NV, cap = sizes
    peers = ny * nz
    gx, gy, gz = lax.axis_index("gx"), lax.axis_index("gy"), lax.axis_index("gz")
    me = gy * nz + gz
    across = [
        {"gx": lax.rem(gx + nx - 1, nx)}, {"gx": lax.rem(gx + 1, nx)},
        {"gy": lax.rem(gy + ny - 1, ny)}, {"gy": lax.rem(gy + 1, ny)},
        {"gz": lax.rem(gz + nz - 1, nz)}, {"gz": lax.rem(gz + 1, nz)},
    ]
    others = []
    for k in range(1, peers):
        p = lax.rem(me + k, peers)
        others.append((p, {"gy": lax.div(p, nz), "gz": lax.rem(p, nz)}))

    barrier = pltpu.get_barrier_semaphore()
    for target in across[:2] + [t for _, t in others]:
        pl.semaphore_signal(barrier, inc=1, device_id=target, device_id_type=MESH)

    lane = iota((Y, Z), 1)
    sub = iota((Y, Z), 0)

    def pack(t, x, values, carry):
        low, high = carry
        for c in range(3):
            at = c * X + x
            low = jnp.where(lane == at, pltpu.roll(values[c], at, 1), low)
            high = jnp.where(lane == at, pltpu.roll(values[c], at + 1, 1), high)
            y_send[t, 0, c, pl.ds(x, 1), :] = values[c][0:1]
            y_send[t, 1, c, pl.ds(x, 1), :] = values[c][Y - 1:Y]
        return low, high

    def fill(x, carry):
        values = [u_in[c, x] for c in range(3)]
        for c in range(3):
            flow[0, c, x + 1] = values[c]
        return pack(0, x, values, carry)

    blank = jnp.zeros((Y, Z), jnp.float32)

    def velocity_copies(t):
        result = []
        for f in range(6):
            s = f % 2
            if f < 2:
                src = flow.at[t, :, X if s else 1]
                dst = flow.at[t, :, 0 if s else X + 1]
            elif f < 4:
                src, dst = y_send.at[t, s], y_recv.at[t, 1 - s]
            else:
                src, dst = z_send.at[t, s], z_recv.at[t, 1 - s]
            result.append(
                pltpu.make_async_remote_copy(
                    src_ref=src, dst_ref=dst, send_sem=v_ssem.at[t, f],
                    recv_sem=v_rsem.at[t, f ^ 1], device_id=across[f], device_id_type=MESH,
                )
            )
        return result

    def trace_copies(t):
        return [
            pltpu.make_async_remote_copy(
                src_ref=tr_send.at[t, f], dst_ref=tr_recv.at[t, f ^ 1],
                send_sem=t_ssem.at[t, f], recv_sem=t_rsem.at[t, f ^ 1],
                device_id=across[f], device_id_type=MESH,
            )
            for f in range(6)
        ]

    def volume_copies(t):
        return [
            pltpu.make_async_remote_copy(
                src_ref=vol_send.at[t, p], dst_ref=vol_recv.at[t, me],
                send_sem=p_ssem.at[t, k], recv_sem=p_rsem.at[t, k],
                device_id=target, device_id_type=MESH,
            )
            for k, (p, target) in enumerate(others)
        ]

    low, high = lax.fori_loop(0, X, fill, (blank, blank))
    z_send[0, 0] = low
    z_send[0, 1] = high
    pl.semaphore_wait(barrier, peers + 1)
    v0 = velocity_copies(0)
    for f in (0, 1, 4, 5, 2, 3):
        v0[f].start()

    L4 = 4 * E
    cell_row = cell_in[...].astype(jnp.float32)
    rows = iota((L4, E), 0)
    cell_rep = jnp.sum(
        jnp.where(iota((L4, E), 1) == rows // 4, cell_row, 0.0), axis=1, keepdims=True
    )
    r = iota((L4, L4), 0)
    l = iota((L4, L4), 1)
    perm = as_float(
        l.astype(jnp.float32) == ((r % 4) * E).astype(jnp.float32) + cell_rep
    ).astype(jnp.bfloat16)
    ah, al = split(ac_in[...].T)
    q_ref[...] = dot(
        jnp.concatenate([ah, al], axis=1), jnp.concatenate([perm, perm], axis=0)
    )

    def trace(f):
        a, s = f // 2, f % 2
        if a == 0:
            return q_ref[s * (K - 1) * FACE:s * (K - 1) * FACE + FACE, :]
        if a == 1:
            base = s * (K - 1) * K
            return jnp.concatenate(
                [q_ref[i * FACE + base:i * FACE + base + K, :] for i in range(K)], axis=0
            )
        return q_ref[pl.ds(s * (K - 1), FACE, stride=K), :]

    def send_traces(t):
        for f in range(6):
            tr_send[t, f] = trace(f).astype(jnp.bfloat16)
        copies = trace_copies(t)
        for copy in copies:
            copy.start()
        return copies

    t0 = send_traces(0)

    cells = VS**3
    own = owner_in[...].astype(jnp.float32)
    own_row = to_row(own, NV)
    matches = (own == own_row) & (iota((NV, NV), 1) < iota((NV, NV), 0))
    rank = jnp.sum(as_float(matches), axis=1, keepdims=True)
    slot_of = own * float(cap) + rank
    W = NV * 2 * VS
    R = peers * cap * VS
    slot_row = spread_row(slot_of, NV, W, 2 * VS)
    wl = iota((1, W), 1)
    goal = slot_row * float(VS) + ((wl % (2 * VS)) // 2).astype(jnp.float32)
    goal = jnp.where(wl % 2 == 0, goal, -1.0)
    place[...] = as_float(iota((R, W), 0).astype(jnp.float32) == goal).astype(jnp.bfloat16)

    slots = peers * cap
    slot_col = to_column(slot_in[...].astype(jnp.float32), slots)
    element_row = spread_row(slot_col, slots, R, VS)
    cell_col = to_column(cell_row, E)
    target_row = jnp.sum(
        jnp.where(iota((E, R), 0).astype(jnp.float32) == element_row, cell_col, 0.0),
        axis=0, keepdims=True,
    )
    goal = target_row + ((iota((1, R), 1) % VS) * E).astype(jnp.float32)
    gather[...] = as_float(iota((VS * E, R), 0).astype(jnp.float32) == goal).astype(jnp.bfloat16)

    PB = VS * Y
    pr = iota((VS * PB, cells), 0)
    pc = iota((VS * PB, cells), 1)
    source_cell = ((pr % PB) // Y * VS + (pr % Y) // 2) * VS + pr // PB
    select = as_float((source_cell == pc) & (pr % 2 == 0)) * (-WAVE_STEP * SOURCE_GAIN)
    arranged = dot(select, proj_in[...], precision=HIGHEST).T
    ph, plo = split(arranged)
    proj_ref[:, :VS * PB] = ph
    proj_ref[:, VS * PB:] = plo

    table = -WAVE_STEP * lobatto_tables(ORDER)
    group3 = iota((K, K, L4), 2) // E
    group2 = iota((FACE, L4), 1) // E
    sub3 = iota((K, K, L4), 1)

    def local_rates():
        factors = []
        subl = iota((K, L4), 0)
        for k in range(K):
            factor = jnp.zeros((K, L4), jnp.float32)
            for c in range(K):
                factor = jnp.where(subl == c, float(table[c, (c - k) % K]), factor)
            factors.append(factor)

        def first(i, carry):
            at = pl.multiple_of(i * FACE, FACE)
            x = q_ref[pl.ds(at, FACE), :].reshape(K, K, L4)
            total = x
            s2 = swap(x, group3, 2, E)
            for k in range(K):
                rolled = s2 if k == 0 else pltpu.roll(s2, k, 1)
                total = total + factors[k][None] * rolled
            s1 = swap(x, group3, 1, E)
            parts = derive([s1[j] for j in range(K)], table)
            total = total + jnp.stack(parts)
            acc[pl.ds(at, FACE), :] = total.reshape(FACE, L4)
            return carry

        lax.fori_loop(0, K, first, 0)

        def second(i, carry):
            ats = [pl.multiple_of(a * FACE + i * K, K) for a in range(K)]
            x = jnp.stack([q_ref[pl.ds(at, K), :] for at in ats])
            s0 = swap(x, group3, 0, E)
            parts = derive([s0[j] for j in range(K)], table)
            for at, part in zip(ats, parts):
                acc[pl.ds(at, K), :] += part
            return carry

        lax.fori_loop(0, K, second, 0)

    lane2 = iota((FACE, L4), 1)
    y_of = (lane2 % E) // EBZ
    z_of = lane2 % EBZ
    scale = WAVE_STEP * 0.5 * ORDER * (ORDER + 1) / 2.0

    def add_flux(t):
        for f in range(6):
            a, s = f // 2, f % 2
            inner = trace(f)
            other = tr_recv[t, f].astype(jnp.float32)
            if a == 0:
                outer = other
            elif a == 1:
                mine = trace(f ^ 1)
                edge = 0 if s else EBY - 1
                mixed = jnp.where(y_of == edge, other, mine)
                near = EBZ if s == 0 else L4 - EBZ
                wrap = (L4 - (EBY - 1) * EBZ) if s == 0 else (EBY - 1) * EBZ
                outer = jnp.where(
                    y_of == (EBY - 1 if s else 0),
                    pltpu.roll(mixed, wrap, 1), pltpu.roll(mixed, near, 1),
                )
            else:
                mine = trace(f ^ 1)
                edge = 0 if s else EBZ - 1
                mixed = jnp.where(z_of == edge, other, mine)
                near = 1 if s == 0 else L4 - 1
                wrap = (L4 - (EBZ - 1)) if s == 0 else EBZ - 1
                outer = jnp.where(
                    z_of == (EBZ - 1 if s else 0),
                    pltpu.roll(mixed, wrap, 1), pltpu.roll(mixed, near, 1),
                )
            jump = inner - outer
            turned = swap(jump, group2, a, E)
            flux = scale * ((turned if s else -turned) - jump)
            if a == 0:
                base = s * (K - 1) * FACE
                acc[base:base + FACE, :] += flux
            elif a == 1:
                base = s * (K - 1) * K
                for i in range(K):
                    at = i * FACE + base
                    acc[at:at + K, :] += flux[i * K:(i + 1) * K]
            else:
                where = pl.ds(s * (K - 1), FACE, stride=K)
                acc[where, :] = acc[where, :] + flux

    def flow_step(t):
        z_low = z_recv[t, 0]
        z_high = z_recv[t, 1]

        def column(x, carry):
            centre = [flow[t, c, x + 1] for c in range(3)]
            below, above = [], []
            for c in range(3):
                at = c * X + x
                u = centre[c]
                pair = (flow[t, c, x], flow[t, c, x + 2])
                y_low = y_recv[t, 0, c, pl.ds(x, 1), :]
                y_high = y_recv[t, 1, c, pl.ds(x, 1), :]
                ym = jnp.where(sub == 0, y_low, pltpu.roll(u, 1, 0))
                yp = jnp.where(sub == Y - 1, y_high, pltpu.roll(u, Y - 1, 0))
                zm = jnp.where(
                    lane == 0, pltpu.roll(z_low, lax.rem(Z - at, Z), 1), pltpu.roll(u, 1, 1)
                )
                zp = jnp.where(
                    lane == Z - 1, pltpu.roll(z_high, Z - 1 - at, 1), pltpu.roll(u, Z - 1, 1)
                )
                below.append((pair[0], ym, zm))
                above.append((pair[1], yp, zp))
            slope = [[0.5 * (above[c][a] - below[c][a]) for c in range(3)] for a in range(3)]
            updated = []
            for c in range(3):
                rate = VISCOSITY * (
                    (above[c][0] + below[c][0])
                    + (above[c][1] + below[c][1])
                    + (above[c][2] + below[c][2])
                    - 6.0 * centre[c]
                )
                for a in range(3):
                    rate = rate - centre[a] * slope[a][c]
                updated.append(centre[c] + FLOW_STEP * rate)
            w = [
                slope[1][2] - slope[2][1], slope[2][0] - slope[0][2], slope[0][1] - slope[1][0]
            ]
            lamb = [
                w[1] * centre[2] - w[2] * centre[1],
                w[2] * centre[0] - w[0] * centre[2],
                w[0] * centre[1] - w[1] * centre[0],
            ]
            if t == 0:
                for c in range(3):
                    flow[1, c, x + 1] = updated[c]
                carry = pack(1, x, updated, carry)
            else:
                for c in range(3):
                    u_out[c, x] = updated[c]
            return lamb, carry

        def couple(i, carry):
            first, carry = column(2 * i, carry)
            second, carry = column(2 * i + 1, carry)
            block = lax.div(i, VS)
            row = lax.rem(i, VS)
            for c in range(3):
                total = first[c] + second[c]
                total = total + pltpu.roll(total, Y - 1, 0)
                total = total + pltpu.roll(total, Z - 1, 1)
                at = pl.multiple_of(c * PB + row * Y, Y)
                lhs[block, pl.ds(at, Y), :] = 0.125 * total
            return carry

        carry = lax.fori_loop(0, X // 2, couple, (blank, blank))
        if t == 0:
            z_send[1, 0] = carry[0]
            z_send[1, 1] = carry[1]

    def send_volumes(t):
        wide = jnp.concatenate([lhs[i] for i in range(X // (2 * VS))], axis=1)
        sent = dot(place[...], wide.astype(jnp.bfloat16), ((1,), (1,)))
        vol_send[t] = sent.astype(vol_send.dtype).reshape(peers, cap * VS, 4 * PB)
        copies = volume_copies(t)
        for copy in copies:
            copy.start()
        vol_recv[t, me] = vol_send[t, me]
        return copies

    def add_source(t):
        received = vol_recv[t].reshape(R, 4 * PB).astype(jnp.bfloat16)
        summed = dot(gather[...], received).T
        group = iota((PB, L4), 1) // E
        blocks = []
        for c in range(VS):
            block = jnp.zeros((PB, L4), jnp.float32)
            for v in range(3):
                part = summed[v * PB:(v + 1) * PB]
                shift = ((1 + v - c) * E) % L4
                if shift:
                    part = pltpu.roll(part, shift, 1)
                block = jnp.where(group == 1 + v, part, block)
            blocks.append(block)
        bh, bl = split(jnp.concatenate(blocks, axis=0))
        source = dot(proj_ref[...], jnp.concatenate([bh, bh], axis=0))
        source = source + dot(proj_ref[:, :VS * PB], bl)
        return acc[...] + source

    lhs[...] = jnp.zeros_like(lhs)
    local_rates()
    for copy in v0:
        copy.wait_recv()
    flow_step(0)
    p0 = send_volumes(0)
    v1 = velocity_copies(1)
    for f in (0, 1, 4, 5, 2, 3):
        v1[f].start()
    for copy in t0:
        copy.wait_recv()
    add_flux(0)
    for copy in v1:
        copy.wait_recv()
    flow_step(1)
    p1 = send_volumes(1)
    for copy in p0:
        copy.wait_recv()
    q_ref[...] = add_source(0)
    t1 = send_traces(1)
    local_rates()
    for copy in t1:
        copy.wait_recv()
    add_flux(1)
    for copy in p1:
        copy.wait_recv()
    final = add_source(1)
    fh, fl = split(final)
    ac_out[...] = dot(
        jnp.concatenate([perm, perm], axis=1), jnp.concatenate([fh, fl], axis=1), ((1,), (1,))
    )
    for copies in (v0, t0, p0, v1, t1, p1):
        for copy in copies:
            copy.wait_send()


def on_device(velocity, acoustic, projection, owner_index, slot_element, element_cell):
    nx, ny, nz = lax.axis_size("gx"), lax.axis_size("gy"), lax.axis_size("gz")
    _, X, Y, Z = velocity.shape
    E = acoustic.shape[0]
    NV = owner_index.shape[0]
    peers = ny * nz
    cap = slot_element.shape[1] // peers
    sizes = (nx, ny, nz, X, Y, Z, E, NV, cap)
    R = peers * cap * VS
    PB = VS * Y
    L4 = 4 * E
    travel = jnp.bfloat16 if (cap * VS) % 16 == 0 else jnp.float32
    vmem = pl.BlockSpec(memory_space=pltpu.VMEM)
    dma = pltpu.SemaphoreType.DMA
    flow, stored = pl.pallas_call(
        functools.partial(kernel, sizes),
        out_shape=(
            jax.ShapeDtypeStruct(velocity.shape, jnp.float32),
            jax.ShapeDtypeStruct((L4, NODES), jnp.float32),
        ),
        in_specs=[vmem] * 6,
        out_specs=(vmem, vmem),
        scratch_shapes=[
            pltpu.VMEM((2, 3, X + 2, Y, Z), jnp.float32),
            pltpu.VMEM((2, 2, 3, X, Z), jnp.float32),
            pltpu.VMEM((2, 2, 3, X, Z), jnp.float32),
            pltpu.VMEM((2, 2, Y, Z), jnp.float32),
            pltpu.VMEM((2, 2, Y, Z), jnp.float32),
            pltpu.VMEM((2, 6, FACE, L4), jnp.bfloat16),
            pltpu.VMEM((2, 6, FACE, L4), jnp.bfloat16),
            pltpu.VMEM((2, peers, cap * VS, 4 * PB), travel),
            pltpu.VMEM((2, peers, cap * VS, 4 * PB), travel),
            pltpu.VMEM((NODES, L4), jnp.float32),
            pltpu.VMEM((NODES, L4), jnp.float32),
            pltpu.VMEM((X // (2 * VS), 4 * PB, Z), jnp.float32),
            pltpu.VMEM((R, NV * 2 * VS), jnp.bfloat16),
            pltpu.VMEM((VS * E, R), jnp.bfloat16),
            pltpu.VMEM((NODES, 2 * VS * PB), jnp.bfloat16),
            dma((2, 6)), dma((2, 6)), dma((2, 6)), dma((2, 6)),
            dma((2, peers - 1)), dma((2, peers - 1)),
        ],
        compiler_params=pltpu.CompilerParams(
            collective_id=0, has_side_effects=True, vmem_limit_bytes=32 * 1024 * 1024
        ),
    )(
        velocity, acoustic.reshape(L4, NODES), projection, owner_index, slot_element, element_cell
    )
    return flow, stored.reshape(acoustic.shape)


def solution(mesh):
    in_specs = (
        P(None, "gx", "gy", "gz"),
        P(("gx", "gy", "gz"), None, None),
        P(),
        P(("gx", "gy", "gz"), None),
        P(("gx", "gy", "gz"), None),
        P(("gx", "gy", "gz"), None),
    )
    out_specs = (P(None, "gx", "gy", "gz"), P(("gx", "gy", "gz"), None, None))
    return jax.shard_map(
        on_device, mesh=mesh, in_specs=in_specs, out_specs=out_specs, check_vma=False
    )
```

profile of v0, /device:TPU:0, one launch (start us, length us, event | category | flops | bytes accessed | tf_op | source)
XLA Modules:
  0.0 26.7 jit_solution(18356682992838525280)
XLA Ops:
  0.6 0.7 %copy.8.owner_in = s32[32,1]{1,0:T(8,128)S(1)} copy(s32[32,1]{0,1:T(1,128)} %param.9) | data formatting | bytes 256 | tf_op args[3]
  1.4 0.0 copy-start
  1.4 0.0 copy-start.1
  1.4 0.0 copy-start.2
  1.4 0.0 copy-start.3
  1.4 1.1 %reshape.10.ac_in = f32[128,512]{1,0:T(8,128)S(1)} reshape(f32[32,4,512]{2,1,0:T(4,128)} %param.7) | data formatting | bytes 524288 | tf_op jit(solution)/shard_map/reshape | solution.py:551
  2.5 0.0 copy-done
  2.5 0.0 copy-done.1
  2.5 0.0 copy-done.2
  2.5 0.0 copy-done.3
  2.5 22.7 %shard_map.77 = (f32[3,16,8,128]{3,2,1,0:T(8,128)S(1)}, f32[128,512]{1,0:T(8,128)S(1)}) custom-call(f32[3,16,8,128]{3,2,1,0:T(8,128)S(1)} %copy-done, f32[128,512]{1,0:T(8,128)S(1)} %reshape.10.ac_in, f32[64,512]{1,0:T(8,128)S(1)} %copy-done.1, s32[32,1]{1,0:T(8,128)S(1)} %copy.8.owner_in, s32[1,64]{1,0:T(1,128)S(1)} %copy-done.2, s32[1,32]{1,0:T(1,128)S(1)} %copy-done.3), custom_call_target="tpu_custom_call" | custom-call | tf_op jit(solution)/shard_map/pallas_call | solution.py:520
  25.3 0.8 %reshape.11 = f32[32,4,512]{2,1,0:T(4,128)} reshape(f32[128,512]{1,0:T(8,128)S(1)} %get-tuple-element.5) | data formatting | bytes 524288 | tf_op jit(solution)/shard_map/reshape | solution.py:553
  26.0 0.7 %copy.10 = f32[3,16,8,128]{3,2,1,0:T(8,128)} copy(f32[3,16,8,128]{3,2,1,0:T(8,128)S(1)} %get-tuple-element.8) | data formatting | bytes 393216
Async XLA Ops:
  1.4 1.1 %copy-start = (f32[3,16,8,128]{3,2,1,0:T(8,128)S(1)}, f32[3,16,8,128]{3,2,1,0:T(8,128)}, u32[]{:S(2)}) copy-start(f32[3,16,8,128]{3,2,1,0:T(8,128)} %u_in.1) | copy-start | bytes 589828
  1.4 1.1 %copy-start.1 = (f32[64,512]{1,0:T(8,128)S(1)}, f32[64,512]{1,0:T(8,128)}, u32[]{:S(2)}) copy-start(f32[64,512]{1,0:T(8,128)} %proj_in.1) | copy-start | bytes 393220
  1.4 1.1 %copy-start.2 = (s32[1,64]{1,0:T(1,128)S(1)}, s32[1,64]{1,0:T(1,128)}, u32[]{:S(2)}) copy-start(s32[1,64]{1,0:T(1,128)} %slot_in.1) | copy-start | bytes 772
  1.4 1.1 %copy-start.3 = (s32[1,32]{1,0:T(1,128)S(1)}, s32[1,32]{1,0:T(1,128)}, u32[]{:S(2)}) copy-start(s32[1,32]{1,0:T(1,128)} %cell_in.1) | copy-start | bytes 388
where the time goes:
time: 26.9 us; the launch traced here: 26.7 us
  Pallas kernels  22.7 us (84%)
  local copies, waits for them, and re-layouts  3.3 us (12%)
  between operations  0.68 us (3%)
    pallas_call x1, Pallas kernels, on_device(): pl.pallas_call(functools.partial(kernel, sizes), out_shape=(jax.ShapeDtyp...  22.7 us
    unnamed x10, local copies, waits for them, and re-layouts  1.43 us
    reshape x1, local copies, waits for them, and re-layouts, on_device(): acoustic.reshape(L4, NODES)  1.09 us
    reshape x1, local copies, waits for them, and re-layouts, on_device(): return (flow, stored.reshape(acoustic.shape))  0.78 us

commit v1 on v0

--- a/solution.py
+++ b/solution.py
@@ -66,11 +66,6 @@
     return jnp.sum(jnp.where(eye, row, 0.0), axis=1, keepdims=True)
 
 
-def to_row(column, count):
-    eye = iota((count, count), 0) == iota((count, count), 1)
-    return jnp.sum(jnp.where(eye, column, 0.0), axis=0, keepdims=True)
-
-
 def spread_row(column, count, width, group):
     pick = iota((count, width), 0) == iota((count, width), 1) // group
     return jnp.sum(jnp.where(pick, column, 0.0), axis=0, keepdims=True)
@@ -86,6 +81,18 @@
     return lax.dot_general(
         a, b, (contract, ((), ())), preferred_element_type=jnp.float32, precision=precision
     )
+
+
+def permutation(cell_row, elements):
+    total = 4 * elements
+    rows = iota((total, elements), 0)
+    cell = jnp.sum(
+        jnp.where(iota((total, elements), 1) == rows % elements, cell_row, 0.0),
+        axis=1, keepdims=True,
+    )
+    r = iota((total, total), 0)
+    goal = (r - r % elements).astype(jnp.float32) + cell
+    return as_float(iota((total, total), 1).astype(jnp.float32) == goal).astype(jnp.bfloat16)
 
 
 def swap(value, group, along, width):
@@ -200,7 +207,7 @@
             for k, (p, target) in enumerate(others)
         ]
 
-    low, high = lax.fori_loop(0, X, fill, (blank, blank))
+    low, high = lax.fori_loop(0, X, fill, (blank, blank), unroll=True)
     z_send[0, 0] = low
     z_send[0, 1] = high
     pl.semaphore_wait(barrier, peers + 1)
@@ -210,16 +217,13 @@
 
     L4 = 4 * E
     cell_row = cell_in[...].astype(jnp.float32)
-    rows = iota((L4, E), 0)
-    cell_rep = jnp.sum(
-        jnp.where(iota((L4, E), 1) == rows // 4, cell_row, 0.0), axis=1, keepdims=True
-    )
-    r = iota((L4, L4), 0)
-    l = iota((L4, L4), 1)
-    perm = as_float(
-        l.astype(jnp.float32) == ((r % 4) * E).astype(jnp.float32) + cell_rep
-    ).astype(jnp.bfloat16)
-    ah, al = split(ac_in[...].T)
+    perm = permutation(cell_row, E)
+    blocks = NODES // L4
+    stored = []
+    for j in range(blocks):
+        parts = [ac_in[pl.ds(4 * j + v, E, stride=4 * blocks), :] for v in range(4)]
+        stored.append(jnp.concatenate(parts, axis=0).T)
+    ah, al = split(jnp.concatenate(stored, axis=0))
     q_ref[...] = dot(
         jnp.concatenate([ah, al], axis=1), jnp.concatenate([perm, perm], axis=0)
     )
@@ -246,8 +250,8 @@
     t0 = send_traces(0)
 
     cells = VS**3
-    own = owner_in[...].astype(jnp.float32)
-    own_row = to_row(own, NV)
+    own_row = owner_in[...].astype(jnp.float32)
+    own = to_column(own_row, NV)
     matches = (own == own_row) & (iota((NV, NV), 1) < iota((NV, NV), 0))
     rank = jnp.sum(as_float(matches), axis=1, keepdims=True)
     slot_of = own * float(cap) + rank
@@ -308,7 +312,7 @@
             acc[pl.ds(at, FACE), :] = total.reshape(FACE, L4)
             return carry
 
-        lax.fori_loop(0, K, first, 0)
+        lax.fori_loop(0, K, first, 0, unroll=True)
 
         def second(i, carry):
             ats = [pl.multiple_of(a * FACE + i * K, K) for a in range(K)]
@@ -319,7 +323,7 @@
                 acc[pl.ds(at, K), :] += part
             return carry
 
-        lax.fori_loop(0, K, second, 0)
+        lax.fori_loop(0, K, second, 0, unroll=True)
 
     lane2 = iota((FACE, L4), 1)
     y_of = (lane2 % E) // EBZ
@@ -433,7 +437,7 @@
                 lhs[block, pl.ds(at, Y), :] = 0.125 * total
             return carry
 
-        carry = lax.fori_loop(0, X // 2, couple, (blank, blank))
+        carry = lax.fori_loop(0, X // 2, couple, (blank, blank), unroll=True)
         if t == 0:
             z_send[1, 0] = carry[0]
             z_send[1, 1] = carry[1]
@@ -465,10 +469,9 @@
         bh, bl = split(jnp.concatenate(blocks, axis=0))
         source = dot(proj_ref[...], jnp.concatenate([bh, bh], axis=0))
         source = source + dot(proj_ref[:, :VS * PB], bl)
-        return acc[...] + source
+        acc[...] = acc[...] + source
 
     lhs[...] = jnp.zeros_like(lhs)
-    local_rates()
     for copy in v0:
         copy.wait_recv()
     flow_step(0)
@@ -476,6 +479,7 @@
     v1 = velocity_copies(1)
     for f in (0, 1, 4, 5, 2, 3):
         v1[f].start()
+    local_rates()
     for copy in t0:
         copy.wait_recv()
     add_flux(0)
@@ -485,22 +489,42 @@
     p1 = send_volumes(1)
     for copy in p0:
         copy.wait_recv()
-    q_ref[...] = add_source(0)
+    add_source(0)
+    q_ref[...] = acc[...]
     t1 = send_traces(1)
     local_rates()
+    for copy in p1:
+        copy.wait_recv()
+    add_source(1)
     for copy in t1:
         copy.wait_recv()
     add_flux(1)
-    for copy in p1:
-        copy.wait_recv()
-    final = add_source(1)
-    fh, fl = split(final)
-    ac_out[...] = dot(
-        jnp.concatenate([perm, perm], axis=1), jnp.concatenate([fh, fl], axis=1), ((1,), (1,))
-    )
+    ac_out[...] = acc[...]
     for copies in (v0, t0, p0, v1, t1, p1):
         for copy in copies:
             copy.wait_send()
+
+
+def finish(u_in, q_in, cell_in, u_hbm, ac_hbm, ac_out, sems):
+    flow_copy = pltpu.make_async_copy(u_in, u_hbm, sems.at[0])
+    flow_copy.start()
+    nodes, total = q_in.shape
+    E = total // 4
+    perm = permutation(cell_in[...].astype(jnp.float32), E)
+    high, low = split(q_in[...])
+    stored = dot(
+        jnp.concatenate([perm, perm], axis=1), jnp.concatenate([high, low], axis=1), ((1,), (1,))
+    )
+    blocks = nodes // total
+    for j in range(blocks):
+        for v in range(4):
+            ac_out[pl.ds(4 * j + v, E, stride=4 * blocks), :] = stored[
+                v * E:(v + 1) * E, j * total:(j + 1) * total
+            ]
+    wave_copy = pltpu.make_async_copy(ac_out, ac_hbm, sems.at[1])
+    wave_copy.start()
+    flow_copy.wait()
+    wave_copy.wait()
 
 
 def on_device(velocity, acoustic, projection, owner_index, slot_element, element_cell):
@@ -516,12 +540,15 @@
     L4 = 4 * E
     travel = jnp.bfloat16 if (cap * VS) % 16 == 0 else jnp.float32
     vmem = pl.BlockSpec(memory_space=pltpu.VMEM)
+    hbm = pl.BlockSpec(memory_space=pltpu.HBM)
     dma = pltpu.SemaphoreType.DMA
-    flow, stored = pl.pallas_call(
+    blocks = NODES // L4
+    cells = acoustic.reshape(E, 4, blocks, L4).transpose(0, 2, 1, 3).reshape(NODES, L4)
+    flow, wave = pl.pallas_call(
         functools.partial(kernel, sizes),
         out_shape=(
             jax.ShapeDtypeStruct(velocity.shape, jnp.float32),
-            jax.ShapeDtypeStruct((L4, NODES), jnp.float32),
+            jax.ShapeDtypeStruct((NODES, L4), jnp.float32),
         ),
         in_specs=[vmem] * 6,
         out_specs=(vmem, vmem),
@@ -548,9 +575,20 @@
             collective_id=0, has_side_effects=True, vmem_limit_bytes=32 * 1024 * 1024
         ),
     )(
-        velocity, acoustic.reshape(L4, NODES), projection, owner_index, slot_element, element_cell
-    )
-    return flow, stored.reshape(acoustic.shape)
+        velocity, cells, projection, owner_index.reshape(1, NV), slot_element, element_cell
+    )
+    flow, stored = pl.pallas_call(
+        finish,
+        out_shape=(
+            jax.ShapeDtypeStruct(velocity.shape, jnp.float32),
+            jax.ShapeDtypeStruct((NODES, L4), jnp.float32),
+        ),
+        in_specs=[vmem] * 3,
+        out_specs=(hbm, hbm),
+        scratch_shapes=[pltpu.VMEM((NODES, L4), jnp.float32), dma((2,))],
+    )(flow, wave, element_cell)
+    stored = stored.reshape(E, blocks, 4, L4).transpose(0, 2, 1, 3).reshape(acoustic.shape)
+    return flow, stored
 
 
 def solution(mesh):

time: 26.9 us -> 28.2 us (1.048)
  local copies, waits for them, and re-layouts: 3.3 us -> 4.81 us
    unnamed x10 -> x16, local copies, waits for them, and re-layouts: 1.43 us -> 4.81 us
    pallas_call x1, Pallas kernels: 22.7 us -> 20.5 us  [on_device(): pl.pallas_call(functools.partial(kernel, sizes), out_shape=(jax.ShapeDtyp...]
    pallas_call x0 -> x1, Pallas kernels: none -> 2.01 us  [on_device(): pl.pallas_call(finish, out_shape=(jax.ShapeDtypeStruct(velocity.shape, jn...]
    reshape x2 -> x0, local copies, waits for them, and re-layouts: 1.86 us -> none  [the longest x1 1.09 us: on_device(): acoustic.reshape(L4, NODES)]
where the time goes in v1:
time: 28.2 us; the launch traced here: 28 us
  Pallas kernels  22.5 us (80%)
  local copies, waits for them, and re-layouts  4.81 us (17%)
  between operations  0.68 us (2%)
    pallas_call x1, Pallas kernels, on_device(): pl.pallas_call(functools.partial(kernel, sizes), out_shape=(jax.ShapeDtyp...  20.5 us
    unnamed x16, local copies, waits for them, and re-layouts  4.81 us
    pallas_call x1, Pallas kernels, on_device(): pl.pallas_call(finish, out_shape=(jax.ShapeDtypeStruct(velocity.shape, jn...  2.01 us

profile of v1, /device:TPU:0, one launch (start us, length us, event | category | flops | bytes accessed | tf_op | source)
XLA Modules:
  0.0 28.0 jit_solution(12856856992267218037)
XLA Ops:
  0.6 0.0 copy-start.5
  0.6 0.0 copy-start.6
  0.7 0.0 copy-start.7
  0.7 0.6 %copy-done.5 = s32[1,32]{1,0:T(1,128)S(1)} copy-done((s32[1,32]{1,0:T(1,128)S(1)}, s32[1,32]{1,0:T(1,128)}, u32[]{:S(2)}) %copy-start.5) | copy-done | bytes 152
  1.3 0.0 copy-done.6
  1.3 0.0 copy-done.7
  1.3 0.0 copy-start.1
  1.3 0.9 %copy-done.1 = f32[32,4,512]{2,1,0:T(4,128)S(1)} copy-done((f32[32,4,512]{2,1,0:T(4,128)S(1)}, f32[32,4,512]{2,1,0:T(4,128)}, u32[]{:S(2)}) %copy-start.1) | copy-done | bytes 262168
  2.3 0.0 copy-start.3
  2.3 0.9 %copy-done.3 = f32[3,16,8,128]{3,2,1,0:T(8,128)S(1)} copy-done((f32[3,16,8,128]{3,2,1,0:T(8,128)S(1)}, f32[3,16,8,128]{3,2,1,0:T(8,128)}, u32[]{:S(2)}) %copy-start.3) | copy-done | bytes 196632
  3.2 0.0 copy-start.4
  3.2 0.9 %copy-done.4 = f32[64,512]{1,0:T(8,128)S(1)} copy-done((f32[64,512]{1,0:T(8,128)S(1)}, f32[64,512]{1,0:T(8,128)}, u32[]{:S(2)}) %copy-start.4) | copy-done | bytes 131096
  4.1 20.5 %shard_map.77 = (f32[3,16,8,128]{3,2,1,0:T(8,128)S(1)}, f32[512,128]{1,0:T(8,128)S(1)}) custom-call(f32[3,16,8,128]{3,2,1,0:T(8,128)S(1)} %copy-done.3, f32[512,128]{1,0:T(8,128)S(1)} %bitcast.11, f32[64,512]{1,0:T(8,128)S(1)} %copy-done.4, s32[1,32]{1,0:T(1,128)S(1)} %bitcast.12, s32[1,64]{1,0:T(1,128)S(1)} %copy-done.7, s32[1,32]{1,0:T(1,128)S(1)} %copy-done.5), custom_call_target="tpu_custom_call" | custom-call | tf_op jit(solution)/shard_map/pallas_call | solution.py:547
  24.6 0.0 copy-start
  24.6 0.7 %copy-done = f32[512,128]{1,0:T(8,128)} copy-done((f32[512,128]{1,0:T(8,128)}, f32[512,128]{1,0:T(8,128)S(1)}, u32[]{:S(2)}) %copy-start) | copy-done | bytes 262168
  25.3 0.0 copy-start.2
  25.3 0.7 %copy-done.2 = f32[3,16,8,128]{3,2,1,0:T(8,128)} copy-done((f32[3,16,8,128]{3,2,1,0:T(8,128)}, f32[3,16,8,128]{3,2,1,0:T(8,128)S(1)}, u32[]{:S(2)}) %copy-start.2) | copy-done | bytes 196632
  26.0 2.0 %shard_map.78 = (f32[3,16,8,128]{3,2,1,0:T(8,128)}, f32[512,128]{1,0:T(8,128)}) custom-call(f32[3,16,8,128]{3,2,1,0:T(8,128)} %copy-done.2, f32[512,128]{1,0:T(8,128)} %copy-done, s32[1,32]{1,0:T(1,128)} %cell_in.3), custom_call_target="tpu_custom_call" | custom-call | tf_op jit(solution)/shard_map/pallas_call | solution.py:580
Async XLA Ops:
  0.6 0.7 %copy-start.5 = (s32[1,32]{1,0:T(1,128)S(1)}, s32[1,32]{1,0:T(1,128)}, u32[]{:S(2)}) copy-start(s32[1,32]{1,0:T(1,128)} %cell_in.3) | copy-start | bytes 388
  0.6 0.7 %copy-start.6 = (s32[32,1]{0,1:T(1,128)S(1)}, s32[32,1]{0,1:T(1,128)}, u32[]{:S(2)}) copy-start(s32[32,1]{0,1:T(1,128)} %param.9) | copy-start | bytes 388
  0.7 0.7 %copy-start.7 = (s32[1,64]{1,0:T(1,128)S(1)}, s32[1,64]{1,0:T(1,128)}, u32[]{:S(2)}) copy-start(s32[1,64]{1,0:T(1,128)} %slot_in.1) | copy-start | bytes 772
  1.3 0.9 %copy-start.1 = (f32[32,4,512]{2,1,0:T(4,128)S(1)}, f32[32,4,512]{2,1,0:T(4,128)}, u32[]{:S(2)}) copy-start(f32[32,4,512]{2,1,0:T(4,128)} %param.7) | copy-start | bytes 786436
  2.3 0.9 %copy-start.3 = (f32[3,16,8,128]{3,2,1,0:T(8,128)S(1)}, f32[3,16,8,128]{3,2,1,0:T(8,128)}, u32[]{:S(2)}) copy-start(f32[3,16,8,128]{3,2,1,0:T(8,128)} %u_in.1) | copy-start | bytes 589828
  3.2 0.9 %copy-start.4 = (f32[64,512]{1,0:T(8,128)S(1)}, f32[64,512]{1,0:T(8,128)}, u32[]{:S(2)}) copy-start(f32[64,512]{1,0:T(8,128)} %proj_in.1) | copy-start | bytes 393220
  24.6 0.7 %copy-start = (f32[512,128]{1,0:T(8,128)}, f32[512,128]{1,0:T(8,128)S(1)}, u32[]{:S(2)}) copy-start(f32[512,128]{1,0:T(8,128)S(1)} %get-tuple-element.7.q_in) | copy-start | bytes 786436
  25.3 0.7 %copy-start.2 = (f32[3,16,8,128]{3,2,1,0:T(8,128)}, f32[3,16,8,128]{3,2,1,0:T(8,128)S(1)}, u32[]{:S(2)}) copy-start(f32[3,16,8,128]{3,2,1,0:T(8,128)S(1)} %get-tuple-element.6.u_in) | copy-start | bytes 589828

commit v2 on v1

--- a/solution.py
+++ b/solution.py
@@ -123,9 +123,9 @@
 
 def kernel(
     sizes,
-    u_in, ac_in, proj_in, owner_in, slot_in, cell_in,
-    u_out, ac_out,
-    flow, y_send, y_recv, z_send, z_recv, tr_send, tr_recv, vol_send, vol_recv,
+    u_hbm, ac_hbm, proj_hbm, owner_hbm, slot_hbm, cell_hbm,
+    u_out, ac_out, perm_out,
+    u_in, ac_in, proj_in, owner_in, slot_in, cell_in, in_sems, flow, y_send, y_recv, z_send, z_recv, tr_send, tr_recv, vol_send, vol_recv,
     q_ref, acc, lhs, place, gather, proj_ref,
     v_ssem, v_rsem, t_ssem, t_rsem, p_ssem, p_rsem,
 ):
@@ -146,6 +146,15 @@
     barrier = pltpu.get_barrier_semaphore()
     for target in across[:2] + [t for _, t in others]:
         pl.semaphore_signal(barrier, inc=1, device_id=target, device_id_type=MESH)
+
+    sources = (u_hbm, cell_hbm, ac_hbm, owner_hbm, slot_hbm, proj_hbm)
+    targets = (u_in, cell_in, ac_in, owner_in, slot_in, proj_in)
+    loads = [
+        pltpu.make_async_copy(src, dst, in_sems.at[i])
+        for i, (src, dst) in enumerate(zip(sources, targets))
+    ]
+    for load in loads:
+        load.start()
 
     lane = iota((Y, Z), 1)
     sub = iota((Y, Z), 0)
@@ -207,6 +216,7 @@
             for k, (p, target) in enumerate(others)
         ]
 
+    loads[0].wait()
     low, high = lax.fori_loop(0, X, fill, (blank, blank), unroll=True)
     z_send[0, 0] = low
     z_send[0, 1] = high
@@ -216,8 +226,11 @@
         v0[f].start()
 
     L4 = 4 * E
+    loads[1].wait()
+    loads[2].wait()
     cell_row = cell_in[...].astype(jnp.float32)
     perm = permutation(cell_row, E)
+    perm_out[...] = perm
     blocks = NODES // L4
     stored = []
     for j in range(blocks):
@@ -250,6 +263,8 @@
     t0 = send_traces(0)
 
     cells = VS**3
+    for load in loads[3:]:
+        load.wait()
     own_row = owner_in[...].astype(jnp.float32)
     own = to_column(own_row, NV)
     matches = (own == own_row) & (iota((NV, NV), 1) < iota((NV, NV), 0))
@@ -505,12 +520,12 @@
             copy.wait_send()
 
 
-def finish(u_in, q_in, cell_in, u_hbm, ac_hbm, ac_out, sems):
+def finish(u_in, q_in, perm_in, u_hbm, ac_hbm, ac_out, sems):
     flow_copy = pltpu.make_async_copy(u_in, u_hbm, sems.at[0])
     flow_copy.start()
     nodes, total = q_in.shape
     E = total // 4
-    perm = permutation(cell_in[...].astype(jnp.float32), E)
+    perm = perm_in[...]
     high, low = split(q_in[...])
     stored = dot(
         jnp.concatenate([perm, perm], axis=1), jnp.concatenate([high, low], axis=1), ((1,), (1,))
@@ -544,15 +559,23 @@
     dma = pltpu.SemaphoreType.DMA
     blocks = NODES // L4
     cells = acoustic.reshape(E, 4, blocks, L4).transpose(0, 2, 1, 3).reshape(NODES, L4)
-    flow, wave = pl.pallas_call(
+    flow, wave, perm = pl.pallas_call(
         functools.partial(kernel, sizes),
         out_shape=(
             jax.ShapeDtypeStruct(velocity.shape, jnp.float32),
             jax.ShapeDtypeStruct((NODES, L4), jnp.float32),
+            jax.ShapeDtypeStruct((L4, L4), jnp.bfloat16),
         ),
-        in_specs=[vmem] * 6,
-        out_specs=(vmem, vmem),
+        in_specs=[hbm] * 6,
+        out_specs=(vmem, vmem, vmem),
         scratch_shapes=[
+            pltpu.VMEM(velocity.shape, jnp.float32),
+            pltpu.VMEM((NODES, L4), jnp.float32),
+            pltpu.VMEM(projection.shape, jnp.float32),
+            pltpu.VMEM((1, NV), jnp.int32),
+            pltpu.VMEM(slot_element.shape, jnp.int32),
+            pltpu.VMEM(element_cell.shape, jnp.int32),
+            dma((6,)),
             pltpu.VMEM((2, 3, X + 2, Y, Z), jnp.float32),
             pltpu.VMEM((2, 2, 3, X, Z), jnp.float32),
             pltpu.VMEM((2, 2, 3, X, Z), jnp.float32),
@@ -575,7 +598,13 @@
             collective_id=0, has_side_effects=True, vmem_limit_bytes=32 * 1024 * 1024
         ),
     )(
-        velocity, cells, projection, owner_index.reshape(1, NV), slot_element, element_cell
+        *[
+            pltpu.with_memory_space_constraint(x, pltpu.HBM)
+            for x in (
+                velocity, cells, projection, owner_index.reshape(1, NV), slot_element,
+                element_cell,
+            )
+        ]
     )
     flow, stored = pl.pallas_call(
         finish,
@@ -586,7 +615,8 @@
         in_specs=[vmem] * 3,
         out_specs=(hbm, hbm),
         scratch_shapes=[pltpu.VMEM((NODES, L4), jnp.float32), dma((2,))],
-    )(flow, wave, element_cell)
+        compiler_params=pltpu.CompilerParams(vmem_limit_bytes=16 * 1024 * 1024),
+    )(flow, wave, perm)
     stored = stored.reshape(E, blocks, 4, L4).transpose(0, 2, 1, 3).reshape(acoustic.shape)
     return flow, stored
 

time: 28.2 us -> 22.4 us (0.79)
  local copies, waits for them, and re-layouts: 4.81 us -> 0 us
  Pallas kernels: 22.5 us -> 21.6 us
    unnamed x16 -> x0, local copies, waits for them, and re-layouts: 4.81 us -> none
    pallas_call x1, Pallas kernels: 2.01 us -> 0.99 us  [on_device(): pl.pallas_call(finish, out_shape=(jax.ShapeDtypeStruct(velocity.shape, jn...]
where the time goes in v2:
time: 22.4 us; the launch traced here: 22.3 us
  Pallas kernels  21.6 us (96%)
  between operations  0.64 us (3%)
    pallas_call x1, Pallas kernels, on_device(): pl.pallas_call(functools.partial(kernel, sizes), out_shape=(jax.ShapeDtyp...  20.6 us
    pallas_call x1, Pallas kernels, on_device(): pl.pallas_call(finish, out_shape=(jax.ShapeDtypeStruct(velocity.shape, jn...  0.99 us

profile of v2, /device:TPU:0, one launch (start us, length us, event | category | flops | bytes accessed | tf_op | source)
XLA Modules:
  0.0 22.3 jit_solution(642202081936395005)
XLA Ops:
  0.6 20.6 %shard_map.77 = (f32[3,16,8,128]{3,2,1,0:T(8,128)S(1)}, f32[512,128]{1,0:T(8,128)S(1)}, bf16[128,128]{1,0:T(8,128)(2,1)S(1)}) custom-call(f32[3,16,8,128]{3,2,1,0:T(8,128)} %u_hbm.1, f32[512,128]{1,0:T(8,128)} %bitcast.11, f32[64,512]{1,0:T(8,128)} %proj_hbm.1, s32[1,32]{1,0:T(1,128)} %bitcast.12, s32[1,64]{1,0:T(1,128)} %slot_hbm.1, s32[1,32]{1,0:T(1,128)} %cell_hbm.1), custom_call_target="tpu_custom_call" | custom-call | tf_op jit(solution)/shard_map/pallas_call | solution.py:562
  21.3 1.0 %shard_map.78 = (f32[3,16,8,128]{3,2,1,0:T(8,128)}, f32[512,128]{1,0:T(8,128)}) custom-call(f32[3,16,8,128]{3,2,1,0:T(8,128)S(1)} %get-tuple-element.7.u_in, f32[512,128]{1,0:T(8,128)S(1)} %get-tuple-element.8.q_in, bf16[128,128]{1,0:T(8,128)(2,1)S(1)} %get-tuple-element.9.perm_in), custom_call_target="tpu_custom_call" | custom-call | tf_op jit(solution)/shard_map/pallas_call | solution.py:609

commit v3 on v2

--- a/solution.py
+++ b/solution.py
@@ -221,9 +221,13 @@
     z_send[0, 0] = low
     z_send[0, 1] = high
     pl.semaphore_wait(barrier, peers + 1)
-    v0 = velocity_copies(0)
-    for f in (0, 1, 4, 5, 2, 3):
-        v0[f].start()
+
+    def send_halos(t):
+        copies = velocity_copies(t)
+        for f in (0, 1, 4, 5, 2, 3):
+            copies[f].start()
+
+    send_halos(0)
 
     L4 = 4 * E
     loads[1].wait()
@@ -255,12 +259,10 @@
     def send_traces(t):
         for f in range(6):
             tr_send[t, f] = trace(f).astype(jnp.bfloat16)
-        copies = trace_copies(t)
-        for copy in copies:
+        for copy in trace_copies(t):
             copy.start()
-        return copies
-
-    t0 = send_traces(0)
+
+    send_traces(0)
 
     cells = VS**3
     for load in loads[3:]:
@@ -430,13 +432,10 @@
                 w[2] * centre[0] - w[0] * centre[2],
                 w[0] * centre[1] - w[1] * centre[0],
             ]
-            if t == 0:
-                for c in range(3):
-                    flow[1, c, x + 1] = updated[c]
-                carry = pack(1, x, updated, carry)
-            else:
-                for c in range(3):
-                    u_out[c, x] = updated[c]
+            for c in range(3):
+                flow[t + 1, c, x + 1] = updated[c]
+                u_out[c, x] = updated[c]
+            carry = pack(t + 1, x, updated, carry)
             return lamb, carry
 
         def couple(i, carry):
@@ -453,19 +452,16 @@
             return carry
 
         carry = lax.fori_loop(0, X // 2, couple, (blank, blank), unroll=True)
-        if t == 0:
-            z_send[1, 0] = carry[0]
-            z_send[1, 1] = carry[1]
+        z_send[t + 1, 0] = carry[0]
+        z_send[t + 1, 1] = carry[1]
 
     def send_volumes(t):
         wide = jnp.concatenate([lhs[i] for i in range(X // (2 * VS))], axis=1)
         sent = dot(place[...], wide.astype(jnp.bfloat16), ((1,), (1,)))
         vol_send[t] = sent.astype(vol_send.dtype).reshape(peers, cap * VS, 4 * PB)
-        copies = volume_copies(t)
-        for copy in copies:
+        for copy in volume_copies(t):
             copy.start()
         vol_recv[t, me] = vol_send[t, me]
-        return copies
 
     def add_source(t):
         received = vol_recv[t].reshape(R, 4 * PB).astype(jnp.bfloat16)
@@ -487,37 +483,48 @@
         acc[...] = acc[...] + source
 
     lhs[...] = jnp.zeros_like(lhs)
-    for copy in v0:
-        copy.wait_recv()
-    flow_step(0)
-    p0 = send_volumes(0)
-    v1 = velocity_copies(1)
-    for f in (0, 1, 4, 5, 2, 3):
-        v1[f].start()
-    local_rates()
-    for copy in t0:
-        copy.wait_recv()
-    add_flux(0)
-    for copy in v1:
-        copy.wait_recv()
-    flow_step(1)
-    p1 = send_volumes(1)
-    for copy in p0:
-        copy.wait_recv()
-    add_source(0)
-    q_ref[...] = acc[...]
-    t1 = send_traces(1)
-    local_rates()
-    for copy in p1:
-        copy.wait_recv()
-    add_source(1)
-    for copy in t1:
-        copy.wait_recv()
-    add_flux(1)
+
+    def arrive(copies):
+        for copy in copies:
+            copy.wait_recv()
+
+    def step(t, carry):
+        arrive(velocity_copies(t))
+        flow_step(t)
+        send_volumes(t)
+
+        @pl.when(t == 0)
+        def _():
+            send_halos(1)
+
+        @pl.when(t == 1)
+        def _():
+            arrive(volume_copies(0))
+            add_source(0)
+            q_ref[...] = acc[...]
+            send_traces(1)
+
+        local_rates()
+
+        @pl.when(t == 1)
+        def _():
+            arrive(volume_copies(1))
+            add_source(1)
+
+        arrive(trace_copies(t))
+        add_flux(t)
+        return carry
+
+    lax.fori_loop(0, 2, step, 0)
     ac_out[...] = acc[...]
-    for copies in (v0, t0, p0, v1, t1, p1):
-        for copy in copies:
-            copy.wait_send()
+
+    def leave(t, carry):
+        for copies in (velocity_copies(t), trace_copies(t), volume_copies(t)):
+            for copy in copies:
+                copy.wait_send()
+        return carry
+
+    lax.fori_loop(0, 2, leave, 0)
 
 
 def finish(u_in, q_in, perm_in, u_hbm, ac_hbm, ac_out, sems):
@@ -576,10 +583,10 @@
             pltpu.VMEM(slot_element.shape, jnp.int32),
             pltpu.VMEM(element_cell.shape, jnp.int32),
             dma((6,)),
-            pltpu.VMEM((2, 3, X + 2, Y, Z), jnp.float32),
+            pltpu.VMEM((3, 3, X + 2, Y, Z), jnp.float32),
+            pltpu.VMEM((3, 2, 3, X, Z), jnp.float32),
             pltpu.VMEM((2, 2, 3, X, Z), jnp.float32),
-            pltpu.VMEM((2, 2, 3, X, Z), jnp.float32),
-            pltpu.VMEM((2, 2, Y, Z), jnp.float32),
+            pltpu.VMEM((3, 2, Y, Z), jnp.float32),
             pltpu.VMEM((2, 2, Y, Z), jnp.float32),
             pltpu.VMEM((2, 6, FACE, L4), jnp.bfloat16),
             pltpu.VMEM((2, 6, FACE, L4), jnp.bfloat16),

time: 22.4 us -> 21.8 us (0.973)
  Pallas kernels: 21.6 us -> 21 us
    pallas_call x1, Pallas kernels: 20.6 us -> 20 us  [on_device(): pl.pallas_call(functools.partial(kernel, sizes), out_shape=(jax.ShapeDtyp...]
where the time goes in v3:
time: 21.8 us; the launch traced here: 21.6 us
  Pallas kernels  21 us (96%)
  between operations  0.64 us (3%)
    pallas_call x1, Pallas kernels, on_device(): pl.pallas_call(functools.partial(kernel, sizes), out_shape=(jax.ShapeDtyp...  20 us
    pallas_call x1, Pallas kernels, on_device(): pl.pallas_call(finish, out_shape=(jax.ShapeDtypeStruct(velocity.shape, jn...  0.99 us

profile of v3, /device:TPU:0, one launch (start us, length us, event | category | flops | bytes accessed | tf_op | source)
XLA Modules:
  0.0 21.6 jit_solution(73674926806734451)
XLA Ops:
  0.6 20.0 %shard_map.77 = (f32[3,16,8,128]{3,2,1,0:T(8,128)S(1)}, f32[512,128]{1,0:T(8,128)S(1)}, bf16[128,128]{1,0:T(8,128)(2,1)S(1)}) custom-call(f32[3,16,8,128]{3,2,1,0:T(8,128)} %u_hbm.1, f32[512,128]{1,0:T(8,128)} %bitcast.11, f32[64,512]{1,0:T(8,128)} %proj_hbm.1, s32[1,32]{1,0:T(1,128)} %bitcast.12, s32[1,64]{1,0:T(1,128)} %slot_hbm.1, s32[1,32]{1,0:T(1,128)} %cell_hbm.1), custom_call_target="tpu_custom_call" | custom-call | tf_op jit(solution)/shard_map/pallas_call | solution.py:569
  20.6 1.0 %shard_map.78 = (f32[3,16,8,128]{3,2,1,0:T(8,128)}, f32[512,128]{1,0:T(8,128)}) custom-call(f32[3,16,8,128]{3,2,1,0:T(8,128)S(1)} %get-tuple-element.7.u_in, f32[512,128]{1,0:T(8,128)S(1)} %get-tuple-element.8.q_in, bf16[128,128]{1,0:T(8,128)(2,1)S(1)} %get-tuple-element.9.perm_in), custom_call_target="tpu_custom_call" | custom-call | tf_op jit(solution)/shard_map/pallas_call | solution.py:616

commit v4 on v3

--- a/solution.py
+++ b/solution.py
@@ -126,7 +126,7 @@
     u_hbm, ac_hbm, proj_hbm, owner_hbm, slot_hbm, cell_hbm,
     u_out, ac_out, perm_out,
     u_in, ac_in, proj_in, owner_in, slot_in, cell_in, in_sems, flow, y_send, y_recv, z_send, z_recv, tr_send, tr_recv, vol_send, vol_recv,
-    q_ref, acc, lhs, place, gather, proj_ref,
+    q_ref, acc, lhs, place, gather, proj_ref, summed, spare,
     v_ssem, v_rsem, t_ssem, t_rsem, p_ssem, p_rsem,
 ):
     nx, ny, nz, X, Y, Z, E, NV, cap = sizes
@@ -147,8 +147,8 @@
     for target in across[:2] + [t for _, t in others]:
         pl.semaphore_signal(barrier, inc=1, device_id=target, device_id_type=MESH)
 
-    sources = (u_hbm, cell_hbm, ac_hbm, owner_hbm, slot_hbm, proj_hbm)
-    targets = (u_in, cell_in, ac_in, owner_in, slot_in, proj_in)
+    sources = (u_hbm, owner_hbm, cell_hbm, ac_hbm, slot_hbm, proj_hbm)
+    targets = (u_in, owner_in, cell_in, ac_in, slot_in, proj_in)
     loads = [
         pltpu.make_async_copy(src, dst, in_sems.at[i])
         for i, (src, dst) in enumerate(zip(sources, targets))
@@ -229,9 +229,23 @@
 
     send_halos(0)
 
+    for load in loads[1:4]:
+        load.wait()
+    own_row = owner_in[...].astype(jnp.float32)
+    own = to_column(own_row, NV)
+    matches = (own == own_row) & (iota((NV, NV), 1) < iota((NV, NV), 0))
+    rank = jnp.sum(as_float(matches), axis=1, keepdims=True)
+    slot_of = own * float(cap) + rank
+    W = NV * 2 * VS
+    slot_row = spread_row(slot_of, NV, W, 2 * VS)
+    wl = iota((1, W), 1)
+    goal = slot_row * float(VS) + ((wl % (2 * VS)) // 2).astype(jnp.float32)
+    goal = jnp.where(wl % 2 == 0, goal, -1.0)
+    place[...] = as_float(
+        iota((peers * cap * VS, W), 0).astype(jnp.float32) == goal
+    ).astype(jnp.bfloat16)
+
     L4 = 4 * E
-    loads[1].wait()
-    loads[2].wait()
     cell_row = cell_in[...].astype(jnp.float32)
     perm = permutation(cell_row, E)
     perm_out[...] = perm
@@ -264,42 +278,37 @@
 
     send_traces(0)
 
+    R = peers * cap * VS
+    PB = VS * Y
     cells = VS**3
-    for load in loads[3:]:
-        load.wait()
-    own_row = owner_in[...].astype(jnp.float32)
-    own = to_column(own_row, NV)
-    matches = (own == own_row) & (iota((NV, NV), 1) < iota((NV, NV), 0))
-    rank = jnp.sum(as_float(matches), axis=1, keepdims=True)
-    slot_of = own * float(cap) + rank
-    W = NV * 2 * VS
-    R = peers * cap * VS
-    slot_row = spread_row(slot_of, NV, W, 2 * VS)
-    wl = iota((1, W), 1)
-    goal = slot_row * float(VS) + ((wl % (2 * VS)) // 2).astype(jnp.float32)
-    goal = jnp.where(wl % 2 == 0, goal, -1.0)
-    place[...] = as_float(iota((R, W), 0).astype(jnp.float32) == goal).astype(jnp.bfloat16)
-
-    slots = peers * cap
-    slot_col = to_column(slot_in[...].astype(jnp.float32), slots)
-    element_row = spread_row(slot_col, slots, R, VS)
-    cell_col = to_column(cell_row, E)
-    target_row = jnp.sum(
-        jnp.where(iota((E, R), 0).astype(jnp.float32) == element_row, cell_col, 0.0),
-        axis=0, keepdims=True,
-    )
-    goal = target_row + ((iota((1, R), 1) % VS) * E).astype(jnp.float32)
-    gather[...] = as_float(iota((VS * E, R), 0).astype(jnp.float32) == goal).astype(jnp.bfloat16)
-
-    PB = VS * Y
-    pr = iota((VS * PB, cells), 0)
-    pc = iota((VS * PB, cells), 1)
-    source_cell = ((pr % PB) // Y * VS + (pr % Y) // 2) * VS + pr // PB
-    select = as_float((source_cell == pc) & (pr % 2 == 0)) * (-WAVE_STEP * SOURCE_GAIN)
-    arranged = dot(select, proj_in[...], precision=HIGHEST).T
-    ph, plo = split(arranged)
-    proj_ref[:, :VS * PB] = ph
-    proj_ref[:, VS * PB:] = plo
+
+    def source_tables():
+        slots = peers * cap
+        slot_col = to_column(slot_in[...].astype(jnp.float32), slots)
+        element_row = spread_row(slot_col, slots, R, VS)
+        cell_col = to_column(cell_row, E)
+        target_row = jnp.sum(
+            jnp.where(iota((E, R), 0).astype(jnp.float32) == element_row, cell_col, 0.0),
+            axis=0, keepdims=True,
+        )
+        goal = target_row + ((iota((1, R), 1) % VS) * E).astype(jnp.float32)
+        gather[...] = as_float(
+            iota((VS * E, R), 0).astype(jnp.float32) == goal
+        ).astype(jnp.bfloat16)
+        blocks = NODES // L4
+        for j in range(blocks):
+            spare[j * cells:(j + 1) * cells, :] = proj_in[:, j * L4:(j + 1) * L4]
+        rows = [
+            jnp.concatenate(
+                [spare[pl.ds(j * cells + c, VS * VS, stride=VS), :] for j in range(blocks)], axis=1
+            )
+            for c in range(VS)
+        ]
+        scaled = (-WAVE_STEP * SOURCE_GAIN) * jnp.concatenate(rows, axis=0)
+        high, low = split(scaled)
+        both = jnp.concatenate([high.astype(jnp.float32), low.astype(jnp.float32)], axis=0)
+        turned = both.T.astype(jnp.bfloat16)
+        proj_ref[...] = jnp.concatenate([turned, turned], axis=1)
 
     table = -WAVE_STEP * lobatto_tables(ORDER)
     group3 = iota((K, K, L4), 2) // E
@@ -465,22 +474,20 @@
 
     def add_source(t):
         received = vol_recv[t].reshape(R, 4 * PB).astype(jnp.bfloat16)
-        summed = dot(gather[...], received).T
-        group = iota((PB, L4), 1) // E
+        summed[...] = dot(gather[...], received).T
+        count = VS * VS
+        group = iota((count, L4), 1) // E
+        parts = [summed[pl.ds(v * PB, count, stride=2), :] for v in range(3)]
         blocks = []
         for c in range(VS):
-            block = jnp.zeros((PB, L4), jnp.float32)
+            block = jnp.zeros((count, L4), jnp.float32)
             for v in range(3):
-                part = summed[v * PB:(v + 1) * PB]
                 shift = ((1 + v - c) * E) % L4
-                if shift:
-                    part = pltpu.roll(part, shift, 1)
+                part = pltpu.roll(parts[v], shift, 1) if shift else parts[v]
                 block = jnp.where(group == 1 + v, part, block)
             blocks.append(block)
-        bh, bl = split(jnp.concatenate(blocks, axis=0))
-        source = dot(proj_ref[...], jnp.concatenate([bh, bh], axis=0))
-        source = source + dot(proj_ref[:, :VS * PB], bl)
-        acc[...] = acc[...] + source
+        high, low = split(jnp.concatenate(blocks, axis=0))
+        acc[...] += dot(proj_ref[...], jnp.concatenate([high, high, low, low], axis=0))
 
     lhs[...] = jnp.zeros_like(lhs)
 
@@ -491,11 +498,18 @@
     def step(t, carry):
         arrive(velocity_copies(t))
         flow_step(t)
-        send_volumes(t)
 
         @pl.when(t == 0)
         def _():
             send_halos(1)
+
+        send_volumes(t)
+
+        @pl.when(t == 0)
+        def _():
+            for load in loads[4:]:
+                load.wait()
+            source_tables()
 
         @pl.when(t == 1)
         def _():
@@ -560,11 +574,11 @@
     R = peers * cap * VS
     PB = VS * Y
     L4 = 4 * E
+    blocks = NODES // L4
     travel = jnp.bfloat16 if (cap * VS) % 16 == 0 else jnp.float32
     vmem = pl.BlockSpec(memory_space=pltpu.VMEM)
     hbm = pl.BlockSpec(memory_space=pltpu.HBM)
     dma = pltpu.SemaphoreType.DMA
-    blocks = NODES // L4
     cells = acoustic.reshape(E, 4, blocks, L4).transpose(0, 2, 1, 3).reshape(NODES, L4)
     flow, wave, perm = pl.pallas_call(
         functools.partial(kernel, sizes),
@@ -597,7 +611,9 @@
             pltpu.VMEM((X // (2 * VS), 4 * PB, Z), jnp.float32),
             pltpu.VMEM((R, NV * 2 * VS), jnp.bfloat16),
             pltpu.VMEM((VS * E, R), jnp.bfloat16),
-            pltpu.VMEM((NODES, 2 * VS * PB), jnp.bfloat16),
+            pltpu.VMEM((NODES, 4 * VS**3), jnp.bfloat16),
+            pltpu.VMEM((4 * PB, L4), jnp.float32),
+            pltpu.VMEM((blocks * VS**3, L4), jnp.float32),
             dma((2, 6)), dma((2, 6)), dma((2, 6)), dma((2, 6)),
             dma((2, peers - 1)), dma((2, peers - 1)),
         ],

time: 21.8 us -> 22.9 us (1.050)
  Pallas kernels: 21 us -> 22.1 us
    pallas_call x1, Pallas kernels: 20 us -> 21.1 us  [on_device(): pl.pallas_call(functools.partial(kernel, sizes), out_shape=(jax.ShapeDtyp...]
where the time goes in v4:
time: 22.9 us; the launch traced here: 22.7 us
  Pallas kernels  22.1 us (97%)
  between operations  0.64 us (3%)
    pallas_call x1, Pallas kernels, on_device(): pl.pallas_call(functools.partial(kernel, sizes), out_shape=(jax.ShapeDtyp...  21.1 us
    pallas_call x1, Pallas kernels, on_device(): pl.pallas_call(finish, out_shape=(jax.ShapeDtypeStruct(velocity.shape, jn...  0.99 us

profile of v4, /device:TPU:0, one launch (start us, length us, event | category | flops | bytes accessed | tf_op | source)
XLA Modules:
  0.0 22.7 jit_solution(14119328553568250601)
XLA Ops:
  0.6 21.1 %shard_map.77 = (f32[3,16,8,128]{3,2,1,0:T(8,128)S(1)}, f32[512,128]{1,0:T(8,128)S(1)}, bf16[128,128]{1,0:T(8,128)(2,1)S(1)}) custom-call(f32[3,16,8,128]{3,2,1,0:T(8,128)} %u_hbm.1, f32[512,128]{1,0:T(8,128)} %bitcast.11, f32[64,512]{1,0:T(8,128)} %proj_hbm.1, s32[1,32]{1,0:T(1,128)} %bitcast.12, s32[1,64]{1,0:T(1,128)} %slot_hbm.1, s32[1,32]{1,0:T(1,128)} %cell_hbm.1), custom_call_target="tpu_custom_call" | custom-call | tf_op jit(solution)/shard_map/pallas_call | solution.py:583
  21.8 1.0 %shard_map.78 = (f32[3,16,8,128]{3,2,1,0:T(8,128)}, f32[512,128]{1,0:T(8,128)}) custom-call(f32[3,16,8,128]{3,2,1,0:T(8,128)S(1)} %get-tuple-element.7.u_in, f32[512,128]{1,0:T(8,128)S(1)} %get-tuple-element.8.q_in, bf16[128,128]{1,0:T(8,128)(2,1)S(1)} %get-tuple-element.9.perm_in), custom_call_target="tpu_custom_call" | custom-call | tf_op jit(solution)/shard_map/pallas_call | solution.py:632

commit v5 on v4

--- a/solution.py
+++ b/solution.py
@@ -495,40 +495,44 @@
         for copy in copies:
             copy.wait_recv()
 
+    def flow_part(k, carry):
+        arrive(velocity_copies(k))
+        flow_step(k)
+
+        @pl.when(k == 0)
+        def _():
+            send_halos(1)
+
+        send_volumes(k)
+        return carry
+
     def step(t, carry):
-        arrive(velocity_copies(t))
-        flow_step(t)
+        local_rates()
 
         @pl.when(t == 0)
         def _():
-            send_halos(1)
-
-        send_volumes(t)
+            lax.fori_loop(0, 2, flow_part, 0)
+
+        @pl.when(t == 1)
+        def _():
+            arrive(volume_copies(1))
+            add_source(1)
+
+        arrive(trace_copies(t))
+        add_flux(t)
 
         @pl.when(t == 0)
-        def _():
-            for load in loads[4:]:
-                load.wait()
-            source_tables()
-
-        @pl.when(t == 1)
         def _():
             arrive(volume_copies(0))
             add_source(0)
             q_ref[...] = acc[...]
             send_traces(1)
 
-        local_rates()
-
-        @pl.when(t == 1)
-        def _():
-            arrive(volume_copies(1))
-            add_source(1)
-
-        arrive(trace_copies(t))
-        add_flux(t)
         return carry
 
+    for load in loads[4:]:
+        load.wait()
+    source_tables()
     lax.fori_loop(0, 2, step, 0)
     ac_out[...] = acc[...]
 

time: 22.9 us -> 23.2 us (1.013)
  Pallas kernels: 22.1 us -> 22.4 us
    pallas_call x1, Pallas kernels: 21.1 us -> 21.5 us  [on_device(): pl.pallas_call(functools.partial(kernel, sizes), out_shape=(jax.ShapeDtyp...]
where the time goes in v5:
time: 23.2 us; the launch traced here: 23.1 us
  Pallas kernels  22.4 us (97%)
  between operations  0.64 us (3%)
    pallas_call x1, Pallas kernels, on_device(): pl.pallas_call(functools.partial(kernel, sizes), out_shape=(jax.ShapeDtyp...  21.5 us
    pallas_call x1, Pallas kernels, on_device(): pl.pallas_call(finish, out_shape=(jax.ShapeDtypeStruct(velocity.shape, jn...  0.99 us

profile of v5, /device:TPU:0, one launch (start us, length us, event | category | flops | bytes accessed | tf_op | source)
XLA Modules:
  0.0 23.1 jit_solution(15886000714574259805)
XLA Ops:
  0.6 21.5 %shard_map.77 = (f32[3,16,8,128]{3,2,1,0:T(8,128)S(1)}, f32[512,128]{1,0:T(8,128)S(1)}, bf16[128,128]{1,0:T(8,128)(2,1)S(1)}) custom-call(f32[3,16,8,128]{3,2,1,0:T(8,128)} %u_hbm.1, f32[512,128]{1,0:T(8,128)} %bitcast.11, f32[64,512]{1,0:T(8,128)} %proj_hbm.1, s32[1,32]{1,0:T(1,128)} %bitcast.12, s32[1,64]{1,0:T(1,128)} %slot_hbm.1, s32[1,32]{1,0:T(1,128)} %cell_hbm.1), custom_call_target="tpu_custom_call" | custom-call | tf_op jit(solution)/shard_map/pallas_call | solution.py:587
  22.1 1.0 %shard_map.78 = (f32[3,16,8,128]{3,2,1,0:T(8,128)}, f32[512,128]{1,0:T(8,128)}) custom-call(f32[3,16,8,128]{3,2,1,0:T(8,128)S(1)} %get-tuple-element.7.u_in, f32[512,128]{1,0:T(8,128)S(1)} %get-tuple-element.8.q_in, bf16[128,128]{1,0:T(8,128)(2,1)S(1)} %get-tuple-element.9.perm_in), custom_call_target="tpu_custom_call" | custom-call | tf_op jit(solution)/shard_map/pallas_call | solution.py:636

commit v6 on v3

--- a/solution.py
+++ b/solution.py
@@ -126,7 +126,7 @@
     u_hbm, ac_hbm, proj_hbm, owner_hbm, slot_hbm, cell_hbm,
     u_out, ac_out, perm_out,
     u_in, ac_in, proj_in, owner_in, slot_in, cell_in, in_sems, flow, y_send, y_recv, z_send, z_recv, tr_send, tr_recv, vol_send, vol_recv,
-    q_ref, acc, lhs, place, gather, proj_ref,
+    q_ref, acc, lhs, place, gather, proj_ref, summed, spare,
     v_ssem, v_rsem, t_ssem, t_rsem, p_ssem, p_rsem,
 ):
     nx, ny, nz, X, Y, Z, E, NV, cap = sizes
@@ -292,14 +292,20 @@
     gather[...] = as_float(iota((VS * E, R), 0).astype(jnp.float32) == goal).astype(jnp.bfloat16)
 
     PB = VS * Y
-    pr = iota((VS * PB, cells), 0)
-    pc = iota((VS * PB, cells), 1)
-    source_cell = ((pr % PB) // Y * VS + (pr % Y) // 2) * VS + pr // PB
-    select = as_float((source_cell == pc) & (pr % 2 == 0)) * (-WAVE_STEP * SOURCE_GAIN)
-    arranged = dot(select, proj_in[...], precision=HIGHEST).T
-    ph, plo = split(arranged)
-    proj_ref[:, :VS * PB] = ph
-    proj_ref[:, VS * PB:] = plo
+    blocks = NODES // L4
+    for j in range(blocks):
+        spare[j * cells:(j + 1) * cells, :] = proj_in[:, j * L4:(j + 1) * L4]
+    rows = [
+        jnp.concatenate(
+            [spare[pl.ds(j * cells + c, VS * VS, stride=VS), :] for j in range(blocks)], axis=1
+        )
+        for c in range(VS)
+    ]
+    scaled = (-WAVE_STEP * SOURCE_GAIN) * jnp.concatenate(rows, axis=0)
+    high, low = split(scaled)
+    both = jnp.concatenate([high.astype(jnp.float32), low.astype(jnp.float32)], axis=0)
+    turned = both.T.astype(jnp.bfloat16)
+    proj_ref[...] = jnp.concatenate([turned, turned], axis=1)
 
     table = -WAVE_STEP * lobatto_tables(ORDER)
     group3 = iota((K, K, L4), 2) // E
@@ -465,22 +471,20 @@
 
     def add_source(t):
         received = vol_recv[t].reshape(R, 4 * PB).astype(jnp.bfloat16)
-        summed = dot(gather[...], received).T
-        group = iota((PB, L4), 1) // E
+        summed[...] = dot(gather[...], received).T
+        count = VS * VS
+        group = iota((count, L4), 1) // E
+        parts = [summed[pl.ds(v * PB, count, stride=2), :] for v in range(3)]
         blocks = []
         for c in range(VS):
-            block = jnp.zeros((PB, L4), jnp.float32)
+            block = jnp.zeros((count, L4), jnp.float32)
             for v in range(3):
-                part = summed[v * PB:(v + 1) * PB]
                 shift = ((1 + v - c) * E) % L4
-                if shift:
-                    part = pltpu.roll(part, shift, 1)
+                part = pltpu.roll(parts[v], shift, 1) if shift else parts[v]
                 block = jnp.where(group == 1 + v, part, block)
             blocks.append(block)
-        bh, bl = split(jnp.concatenate(blocks, axis=0))
-        source = dot(proj_ref[...], jnp.concatenate([bh, bh], axis=0))
-        source = source + dot(proj_ref[:, :VS * PB], bl)
-        acc[...] = acc[...] + source
+        high, low = split(jnp.concatenate(blocks, axis=0))
+        acc[...] += dot(proj_ref[...], jnp.concatenate([high, high, low, low], axis=0))
 
     lhs[...] = jnp.zeros_like(lhs)
 
@@ -560,11 +564,11 @@
     R = peers * cap * VS
     PB = VS * Y
     L4 = 4 * E
+    blocks = NODES // L4
     travel = jnp.bfloat16 if (cap * VS) % 16 == 0 else jnp.float32
     vmem = pl.BlockSpec(memory_space=pltpu.VMEM)
     hbm = pl.BlockSpec(memory_space=pltpu.HBM)
     dma = pltpu.SemaphoreType.DMA
-    blocks = NODES // L4
     cells = acoustic.reshape(E, 4, blocks, L4).transpose(0, 2, 1, 3).reshape(NODES, L4)
     flow, wave, perm = pl.pallas_call(
         functools.partial(kernel, sizes),
@@ -597,7 +601,9 @@
             pltpu.VMEM((X // (2 * VS), 4 * PB, Z), jnp.float32),
             pltpu.VMEM((R, NV * 2 * VS), jnp.bfloat16),
             pltpu.VMEM((VS * E, R), jnp.bfloat16),
-            pltpu.VMEM((NODES, 2 * VS * PB), jnp.bfloat16),
+            pltpu.VMEM((NODES, 4 * VS**3), jnp.bfloat16),
+            pltpu.VMEM((4 * PB, L4), jnp.float32),
+            pltpu.VMEM((blocks * VS**3, L4), jnp.float32),
             dma((2, 6)), dma((2, 6)), dma((2, 6)), dma((2, 6)),
             dma((2, peers - 1)), dma((2, peers - 1)),
         ],

time: 21.8 us -> 21.7 us (level)
  no operation moved by 1% of the time
where the time goes in v6:
time: 21.7 us; the launch traced here: 21.6 us
  Pallas kernels  20.9 us (96%)
  between operations  0.64 us (3%)
    pallas_call x1, Pallas kernels, on_device(): pl.pallas_call(functools.partial(kernel, sizes), out_shape=(jax.ShapeDtyp...  20 us
    pallas_call x1, Pallas kernels, on_device(): pl.pallas_call(finish, out_shape=(jax.ShapeDtypeStruct(velocity.shape, jn...  0.99 us

profile of v6, /device:TPU:0, one launch (start us, length us, event | category | flops | bytes accessed | tf_op | source)
XLA Modules:
  0.0 21.6 jit_solution(731091701501074576)
XLA Ops:
  0.6 20.0 %shard_map.77 = (f32[3,16,8,128]{3,2,1,0:T(8,128)S(1)}, f32[512,128]{1,0:T(8,128)S(1)}, bf16[128,128]{1,0:T(8,128)(2,1)S(1)}) custom-call(f32[3,16,8,128]{3,2,1,0:T(8,128)} %u_hbm.1, f32[512,128]{1,0:T(8,128)} %bitcast.11, f32[64,512]{1,0:T(8,128)} %proj_hbm.1, s32[1,32]{1,0:T(1,128)} %bitcast.12, s32[1,64]{1,0:T(1,128)} %slot_hbm.1, s32[1,32]{1,0:T(1,128)} %cell_hbm.1), custom_call_target="tpu_custom_call" | custom-call | tf_op jit(solution)/shard_map/pallas_call | solution.py:573
  20.6 1.0 %shard_map.78 = (f32[3,16,8,128]{3,2,1,0:T(8,128)}, f32[512,128]{1,0:T(8,128)}) custom-call(f32[3,16,8,128]{3,2,1,0:T(8,128)S(1)} %get-tuple-element.7.u_in, f32[512,128]{1,0:T(8,128)S(1)} %get-tuple-element.8.q_in, bf16[128,128]{1,0:T(8,128)(2,1)S(1)} %get-tuple-element.9.perm_in), custom_call_target="tpu_custom_call" | custom-call | tf_op jit(solution)/shard_map/pallas_call | solution.py:622
